TPU v7x, 32 devices: a whole 2x2x4 slice. The times are simulated.
32 devices in a mesh: cls: 2 (over core), ptcl: 16 (over z, y, x).
Axes of the slice: x: 2, y: 2, z: 4, core: 2. Of those that a mesh axis runs over, the one named last changes fastest.
Arguments:
- particles: bfloat16 [16384, 2048], P('ptcl')
- panels: bfloat16 [2, 128, 2048], P('cls', 'ptcl')
- sigma2: float32 [32], replicated, may hold values from 0.5 to 2
- defocus_bins: int32 [16384], P('ptcl'), may hold values from 0 to 15
- half_sets: int32 [16384], P('ptcl'), may hold values 0 or 1
- prior_mask: int32 [16384, 2], P('ptcl', 'cls'), may hold values from 0 to 1, as said below
- orient_ids: int32 [128], replicated, may hold values from 0 to 127, each once
Outputs:
- half_maps: float32 [2, 256, 2048], P('cls', 'ptcl')
- log_evidence: float32 [16384], P('ptcl')
Inputs may be any that keep to these rules, and one draw needn't show every extreme that they name: `prior_mask`: every particle allows at least one class. `orient_ids`: each direction 0 to 127 appears once.
All inputs are finite; a program needn't handle non-finite values. No bound on the sum of `half_sets` on one device may be relied on, other than what follows from the above.
Results may differ from a plain program's by a relative error of at most 0.0015.
The roundings to bfloat16 on the way count: a program that leaves them out, or rounds other values in their place, can miss the bound.
Values may be sent and summed in bfloat16 or wider, within the bound.
A program may use at most 64 MiB of HBM per device.

v0:
```python
import jax
import jax.numpy as jnp
from jax import lax
from jax.sharding import PartitionSpec as P

PIXC = 1024
ORIENT = 128
NSHELL = 32
NBIN = 16


def from_partner(shard, axis, apart):
    return lax.ppermute(shard, axis, [(i, i ^ 1 << apart) for i in range(lax.axis_size(axis))])


def ctf_table():
    bins = jnp.arange(NBIN, dtype=jnp.float32)
    defocus = (bins + 1.0) / NBIN
    radius = (jnp.arange(PIXC, dtype=jnp.float32) + 0.5) / PIXC
    phase = 0.3 + 2.5 * defocus[:, None] * radius[None, :]
    return jnp.sin(phase) + 0.1 * jnp.cos(phase)


def lookup_small(indices, values):
    count = values.shape[0]
    match = indices[:, None] == jnp.arange(count, dtype=jnp.int32)[None, :]
    return jnp.sum(jnp.where(match, values[None, :], 0.0), axis=1)


def contract_rows(left, right):
    return lax.dot_general(
        left, right, (((0,), (0,)), ((), ())), preferred_element_type=jnp.float32
    )


def on_device(particles, panels, sigma2, defocus_bins, half_sets, prior_mask, orient_ids):
    shells = jnp.arange(PIXC, dtype=jnp.int32) * NSHELL // PIXC
    inverse_noise = lookup_small(shells, 1.0 / sigma2)
    table = ctf_table()
    onehot_bin = (defocus_bins[:, None] == jnp.arange(NBIN, dtype=jnp.int32)[None, :]).astype(
        jnp.float32
    )
    contrast = jnp.dot(onehot_bin, table, precision=lax.Precision.HIGHEST)
    doubled = jnp.concatenate([contrast, contrast], axis=1)
    noise_pair = jnp.concatenate([inverse_noise, inverse_noise])
    images = particles.astype(jnp.float32)
    weighted = (images * doubled * noise_pair[None, :]).astype(jnp.bfloat16)
    power = (contrast * contrast * inverse_noise[None, :]).astype(jnp.bfloat16)
    piece = lax.all_gather(panels[0], "ptcl", axis=0, tiled=True)
    piece_f = piece.astype(jnp.float32)
    piece_power = (piece_f[:, :PIXC] ** 2 + piece_f[:, PIXC:] ** 2).astype(jnp.bfloat16)
    direct = lax.dot_general(
        weighted, piece, (((1,), (1,)), ((), ())), preferred_element_type=jnp.float32
    )
    norm_part = lax.dot_general(
        power, piece_power, (((1,), (1,)), ((), ())), preferred_element_type=jnp.float32
    )
    scores = direct - 0.5 * norm_part
    allowed = (prior_mask[:, 0] > 0)[:, None]
    masked = jnp.where(allowed, scores, -1e30)
    local_peak = jnp.max(masked, axis=1)
    peak = lax.pmax(local_peak, "cls")
    weights_exp = jnp.where(allowed, jnp.exp(masked - peak[:, None]), 0.0)
    total = lax.psum(jnp.sum(weights_exp, axis=1), "cls")
    log_evidence = peak + jnp.log(total)
    posterior = (weights_exp / total[:, None]).astype(jnp.bfloat16)
    permuter = (orient_ids[:, None] == jnp.arange(ORIENT, dtype=jnp.int32)[None, :]).astype(
        jnp.bfloat16
    )
    by_direction = jnp.dot(posterior, permuter, preferred_element_type=jnp.float32).astype(
        jnp.bfloat16
    )
    half_col = half_sets.astype(jnp.bfloat16)[:, None]
    split_post = jnp.concatenate([by_direction * (1 - half_col), by_direction * half_col], axis=1)
    centred = (images * doubled).astype(jnp.bfloat16)
    squares_ctf = (contrast * contrast).astype(jnp.bfloat16)
    stacked = jnp.concatenate([centred, squares_ctf], axis=1)
    summed = lax.psum_scatter(
        contract_rows(split_post, stacked), "ptcl", scatter_dimension=0, tiled=True
    )
    data = summed[:, : 2 * PIXC]
    weight = summed[:, 2 * PIXC :]
    top_bit = lax.axis_size("ptcl").bit_length() - 2
    partner = from_partner(data.astype(jnp.bfloat16), "ptcl", top_bit).astype(data.dtype)
    half_index = lax.axis_index("ptcl") // (lax.axis_size("ptcl") // 2)

    def per_shell(values):
        summed_rows = jnp.sum(values, axis=0)
        folded = summed_rows[:PIXC] + summed_rows[PIXC:]
        return jnp.sum(folded.reshape(NSHELL, PIXC // NSHELL), axis=1)

    cross = per_shell(data * partner)
    own_power = per_shell(data * data)
    is_first = half_index == 0
    stats = jnp.stack(
        [0.5 * cross, jnp.where(is_first, own_power, 0.0), jnp.where(is_first, 0.0, own_power)]
    )
    totals = lax.psum(stats, "ptcl")
    fsc = totals[0] / jnp.sqrt(totals[1] * totals[2] + 1e-06)
    factor = (1.0 + lookup_small(shells, fsc)) / 2.0
    factor_pair = jnp.concatenate([factor, factor])
    weight_pair = jnp.concatenate([weight, weight], axis=1)
    half_maps = data * factor_pair[None, :] / (weight_pair + 1.0)
    return (half_maps[None], log_evidence)


def solution(mesh):
    placed = (
        P("ptcl", None),
        P("cls", "ptcl", None),
        P(),
        P("ptcl"),
        P("ptcl"),
        P("ptcl", "cls"),
        P(),
    )
    return jax.shard_map(
        on_device,
        mesh=mesh,
        in_specs=placed,
        out_specs=(P("cls", "ptcl", None), P("ptcl")),
        check_vma=False,
    )
```

profile of v0, /device:TPU:0, one launch (start us, length us, event | category | flops | bytes accessed | tf_op | source)
XLA Modules:
  0.0 261.6 jit_solution(6150940914794436655)
XLA Ops:
  7.3 0.7 broadcast_divide_fusion
  8.0 6.4 %copy.10 = bf16[1024,2048]{0,1:T(8,128)(2,1)} copy(bf16[1024,2048]{1,0:T(8,128)(2,1)} %param.7) | data formatting | bytes 8388608 | tf_op args[0]
  14.5 45.5 %all-gather = bf16[1,128,2048]{2,1,0:T(8,128)(2,1)S(1)} all-gather(bf16[1,8,2048]{2,1,0:T(8,128)(2,1)S(1)} %copy-done.1), channel_id=2, replica_groups=mesh['cls'=2,'ptcl'=16] {'ptcl'}, dimensions={1}, use_global_device_ids=true | all-gather | bytes 557056 | tf_op jit(solution)/shard_map/all_gather | solution.py:49
  59.9 0.1 bitcast_convert_fusion
  60.0 2.2 multiply_convert_fusion.3
  62.3 3.2 %fusion = bf16[1024,2048]{0,1:T(8,128)(2,1)} fusion(f32[1024,1024]{0,1:T(8,128)S(1)} %get-tuple-element.11, bf16[1024,2048]{0,1:T(8,128)(2,1)S(1)} %copy-done), kind=kLoop, calls=%fused_computation.2 | loop fusion | flops 8388608 | bytes 12582912 | tf_op jit(solution)/shard_map/convert_element_type | solution.py:75
  65.5 1.4 fusion.5
  67.0 0.7 fusion.45
  67.7 2.5 pmax.7
  70.2 0.1 fusion.18
  70.3 2.5 psum.14
  72.8 0.3 broadcast_multiply_fusion.1
  73.1 5.8 %fusion.1 = f32[256,3072]{1,0:T(8,128)} fusion(bf16[1024,1024]{0,1:T(8,128)(2,1)S(1)} %get-tuple-element.10, bf16[1024,2048]{0,1:T(8,128)(2,1)} %fusion, bf16[1024,128]{0,1:T(8,128)(2,1)S(1)} %get-tuple-element.7, bf16[1024,128]{0,1:T(8,128)(2,1)S(1)} %get-tuple-element.6), kind=kOutput, calls=%fused_computation.3 | convolution fusion | flops 1624244224 | bytes 9961472 | tf_op jit(solution)/shard_map/dot_general | solution.py:31
  78.9 126.8 %reduce-scatter.2.cloned.1.call-done = f32[16,3072]{1,0:T(8,128)} async-done(((f32[256,3072]{1,0:T(8,128)}), f32[16,3072]{1,0:T(8,128)}) %reduce-scatter.2.cloned.1.call-update) | async-done | bytes 196624 | tf_op jit(solution)/shard_map/reduce_scatter | solution.py:78
  205.8 0.9 slice.105
  206.7 1.6 collective-permute-start
  208.3 0.6 log_add_fusion
  208.9 0.8 slice.83
  209.7 2.1 collective-permute-done
  211.8 1.0 multiply_reduce_fusion.1
  212.9 0.1 reduce_sum.68
  213.1 0.1 reduce_sum.66
  213.2 39.8 %psum.15 = f32[3,32]{1,0:T(4,128)S(1)} all-reduce(f32[3,32]{1,0:T(4,128)S(1)} %pad_maximum_fusion.2), channel_id=1, replica_groups=mesh['cls'=2,'ptcl'=16] {'ptcl'}, use_global_device_ids=true, to_apply=%region_10.11 | all-reduce | flops 96 | bytes 768 | tf_op jit(solution)/shard_map/psum | solution.py:98
  253.2 1.6 fusion.23
  (31 shorter events, 0.5 us)
Async XLA Ops:
  7.2 198.6 %reduce-scatter.2.cloned.1.call-start = ((), (), s32[]{:S(2)}) async-start(), calls=%async_computation.1 | async-start | bytes 3342336 | tf_op jit(solution)/shard_map/reduce_scatter | solution.py:78
  8.0 6.4 %copy-start.1 = (bf16[1,8,2048]{2,1,0:T(8,128)(2,1)S(1)}, bf16[1,8,2048]{2,1,0:T(8,128)(2,1)}, u32[]{:S(2)}) copy-start(bf16[1,8,2048]{2,1,0:T(8,128)(2,1)} %param.8) | copy-start | bytes 98308
  8.0 52.0 %copy-start.2 = (s32[1024]{0:T(1024)S(1)}, s32[1024]{0:T(1024)}, u32[]{:S(2)}) copy-start(s32[1024]{0:T(1024)} %param.10) | copy-start | bytes 12292
  14.5 47.8 %copy-start = (bf16[1024,2048]{0,1:T(8,128)(2,1)S(1)}, bf16[1024,2048]{0,1:T(8,128)(2,1)}, u32[]{:S(2)}) copy-start(bf16[1024,2048]{0,1:T(8,128)(2,1)} %copy.10) | copy-start | bytes 12582916
  65.5 1.4 copy-start.3
  67.0 5.8 %copy-start.4 = (s32[1024]{0:T(1024)S(1)}, s32[1024]{0:T(1024)}, u32[]{:S(2)}) copy-start(s32[1024]{0:T(1024)} %param.11) | copy-start | bytes 12292
  67.0 5.8 %copy-start.5 = (s32[128]{0:T(128)S(1)}, s32[128]{0:T(128)}, u32[]{:S(2)}) copy-start(s32[128]{0:T(128)} %param.13) | copy-start | bytes 1540
  206.7 5.2 %collective-permute-start = (bf16[16,2048]{1,0:T(8,128)(2,1)S(1)}, bf16[16,2048]{1,0:T(8,128)(2,1)S(1)}, u32[]{:S(2)}, u32[]{:S(2)}) collective-permute-start(bf16[16,2048]{1,0:T(8,128)(2,1)S(1)} %slice.105), channel_id=1, source_target_pairs={{0,8},{1,9},{2,10},{3,11},{4,12},{5,13},{6,14},{7,15},{8,0},{9,1},... | collective-permute-start | bytes 196616 | tf_op jit(solution)/shard_map/ppermute | solution.py:13
Sparse Core Ops, SparseCore 0:
  79.0 126.6 reduce-scatter.1
where the time goes:
time: 262 us
  waiting for transfers between devices  129 us (49%)
  blocking collectives  90.3 us (34%)
  between operations  14.2 us (5%)
  matrix products  10.4 us (4%)
  local copies, waits for them, and re-layouts  8.34 us (3%)
  other arithmetic  7.76 us (3%)
    reduce_scatter x1, waiting for transfers between devices, on_device(): lax.psum_scatter(contract_rows(split_post, stacked), 'ptcl', scatter_dime...  127 us
    all_gather x1, blocking collectives, on_device(): piece = lax.all_gather(panels[0], 'ptcl', axis=0, tiled=True)  45.5 us
    psum x1, blocking collectives, on_device(): totals = lax.psum(stats, 'ptcl')  39.8 us
    unnamed x13, local copies, waits for them, and re-layouts  6.44 us
    dot_general x1, matrix products, contract_rows(): lax.dot_general(left, right, (((0,), (0,)), ((), ())), preferred_element_...  5.75 us
  transfers between devices with their start and end apart: 2, of which 2 were waited for; matrix products, arithmetic and copies ran while one was open for 1% of the time, Pallas kernels for 0%

commit v1 on v0

v1 whole, which is shorter than its diff:
```python
import functools

import jax
import jax.numpy as jnp
import numpy as np
from jax import lax
from jax.experimental import pallas as pl
from jax.experimental.pallas import tpu as pltpu
from jax.sharding import PartitionSpec as P

PIXC = 1024
ORIENT = 128
NSHELL = 32
NBIN = 16
LANES = 128
WIDTH = 2 * PIXC + LANES
CHUNKS = ((1536, 640), (0, 512), (512, 512), (1024, 512))
MESH = pl.DeviceIdType.MESH
BF16 = jnp.bfloat16
F32 = jnp.float32


def ctf_table():
    defocus = (np.arange(NBIN, dtype=np.float32) + np.float32(1.0)) / np.float32(NBIN)
    radius = (np.arange(PIXC, dtype=np.float32) + np.float32(0.5)) / np.float32(PIXC)
    phase = np.float32(0.3) + np.float32(2.5) * defocus[:, None] * radius[None, :]
    wide = phase.astype(np.float64)
    return (np.sin(wide) + 0.1 * np.cos(wide)).astype(np.float32)


def iota(shape, dim):
    return lax.broadcasted_iota(jnp.int32, shape, dim)


def dot(left, right):
    return lax.dot_general(left, right, (((1,), (0,)), ((), ())), preferred_element_type=F32)


def dot_t(left, right):
    return lax.dot_general(left, right, (((1,), (1,)), ((), ())), preferred_element_type=F32)


def split3(values):
    high = values.astype(BF16)
    rest = values - high.astype(F32)
    mid = rest.astype(BF16)
    low = (rest - mid.astype(F32)).astype(BF16)
    return high, mid, low


def exact(values, product):
    high, mid, low = split3(values)
    return product(high) + product(mid) + product(low)


def by_group(values, dim):
    high, mid, low = split3(values)
    group = iota(values.shape, dim) // NBIN
    mixed = jnp.where(
        group == 0,
        high.astype(F32),
        jnp.where(group == 1, mid.astype(F32), jnp.where(group == 2, low.astype(F32), 0.0)),
    )
    return mixed.astype(BF16)


def kernel(
    dims,
    particles,
    panels,
    sigma2,
    bins,
    halves,
    prior,
    orient,
    table,
    maps,
    evidence,
    images,
    weighted,
    centred,
    gathered,
    onehot,
    tables,
    noise,
    peaks,
    posts,
    send1,
    recv1,
    acc,
    recv2,
    final,
    swapped,
    stats,
    load_sem,
    gsend,
    grecv,
    csend,
    crecv,
    s1send,
    s1recv,
    s2send,
    s2recv,
    xsend,
    xrecv,
    tsend,
    trecv,
):
    n, ncls, plane, line, rows, pad, count = dims
    block = 2 * pad
    total_rows = n * block
    own_rows = line * block
    me = lax.axis_index("ptcl")
    mine = lax.axis_index("cls")
    q = lax.rem(me, plane)
    l = me // plane
    half = me // (n // 2)

    def at(line_pos, plane_pos):
        return line_pos * plane + plane_pos

    def remote(src, dst, send, recv, ptcl=None, cls=None):
        return pltpu.make_async_remote_copy(
            src_ref=src,
            dst_ref=dst,
            send_sem=send,
            recv_sem=recv,
            device_id=(mine if cls is None else cls, me if ptcl is None else ptcl),
            device_id_type=MESH,
        )

    barrier = pltpu.get_barrier_semaphore()
    for i in range(1, n):
        pl.semaphore_signal(
            barrier, inc=1, device_id=(mine, lax.rem(me + i, n)), device_id_type=MESH
        )
    for i in range(1, ncls):
        pl.semaphore_signal(
            barrier, inc=1, device_id=(lax.rem(mine + i, ncls), me), device_id_type=MESH
        )
    quarter = count // 4
    loads = []
    for i in range(4):
        span = pl.ds(i * quarter, quarter)
        loads.append(
            pltpu.make_async_copy(particles.at[span], images.at[span], load_sem.at[i])
        )
        loads[-1].start()

    piece = panels[0].astype(F32)
    real, imag = piece[:, :PIXC], piece[:, PIXC:]
    if rows < pad:
        fill = jnp.zeros((pad - rows, PIXC), F32)
        parts = [real, fill, imag, fill]
    else:
        parts = [real, imag]

    def spot(device):
        return gathered.at[pl.ds(pl.multiple_of(device * block, block), block)]

    gathered[pl.ds(pl.multiple_of(me * block, block), block), :] = jnp.concatenate(
        parts, axis=0
    ).astype(BF16)
    pl.semaphore_wait(barrier, n - 1 + ncls - 1)

    sends = []
    line_copies = [None]
    for i in range(1, line):
        copy = remote(
            spot(me), spot(me), gsend.at[i, 0], grecv.at[i, 0], at(lax.rem(l + i, line), q)
        )
        copy.start()
        line_copies.append(copy)
    plane_copies = []

    def forward(i):
        source = at(lax.rem(l + line - i, line), q)
        for p in range(1, plane):
            copy = remote(
                spot(source),
                spot(source),
                gsend.at[i, p],
                grecv.at[i, p],
                at(l, lax.rem(q + p, plane)),
            )
            copy.start()
            plane_copies.append(copy)

    forward(0)

    shell_pick = (iota((LANES, PIXC), 0) == iota((LANES, PIXC), 1) // (PIXC // NSHELL)).astype(
        F32
    ).astype(BF16)
    inverse = jnp.broadcast_to(1.0 / sigma2[...], (8, NSHELL))
    noise[...] = exact(inverse, lambda v: dot(v, shell_pick[:NSHELL]))
    base = table[...]
    base = jnp.concatenate(
        [base, base, base, jnp.zeros((LANES - 3 * NBIN, PIXC), F32)], axis=0
    )
    tables[0] = by_group(base, 0)
    tables[1] = (base * base * noise[0:1, :]).astype(BF16)
    tables[2] = (base * base).astype(BF16)
    row = iota((LANES, count), 0)
    onehot[...] = (
        jnp.where((row < 3 * NBIN) & (lax.rem(row, NBIN) == bins[...]), 1.0, 0.0)
    ).astype(BF16)

    step = LANES

    def prepare(first, last):
        def body(i, carry):
            span = pl.ds(pl.multiple_of(i * step, step), step)
            picks = onehot[:, span]
            contrast = lax.dot_general(
                picks, tables[0], (((0,), (0,)), ((), ())), preferred_element_type=F32
            )
            level = noise[0:1, :]
            for part in range(2):
                cols = slice(part * PIXC, (part + 1) * PIXC)
                product = images[span, cols].astype(F32) * contrast
                centred[span, cols] = product.astype(BF16)
                weighted[span, cols] = (product * level).astype(BF16)
            return carry

        lax.fori_loop(first, last, body, 0)

    per = quarter // step
    for i in range(4):
        loads[i].wait()
        if i == 2:
            for s in range(1, line):
                line_copies[s].wait_recv()
                forward(s)
        prepare(i * per, (i + 1) * per)

    ids = jnp.broadcast_to(orient[...].astype(F32), (8, ORIENT)).astype(BF16)
    shape = (ORIENT, total_rows)
    col = iota(shape, 1)
    within = lax.rem(col, pad)
    expand = jnp.where(
        (col // block * rows + within == iota(shape, 0)) & (within < rows), 1.0, 0.0
    ).astype(BF16)
    ids_cols = dot(ids, expand)[0:1, :]
    square = (total_rows, total_rows)
    r = iota((total_rows, 1), 0)
    slot = lax.rem(r, pad)
    r_line = lax.rem(lax.rem(r // block, line) + l, line)
    r_plane = lax.rem(r // own_rows + q, plane)
    owner = at(r_line, r_plane)
    pairs = n // 2
    direction = lax.rem(owner, pairs) * (2 * rows) + owner // pairs * rows + slot
    direction = jnp.where(slot < rows, direction, -1).astype(F32)
    c = iota((1, total_rows), 1)
    c_part = lax.rem(c // pad, 2)
    c_ok = lax.rem(c, pad) < rows
    real_ids = jnp.where(c_ok & (c_part == 0), ids_cols, -2.0)
    imag_ids = jnp.where(c_ok & (c_part == 1), ids_cols, -2.0)
    pick_real = jnp.where(jnp.broadcast_to(direction, square) == real_ids, 1.0, 0.0).astype(BF16)
    pick_imag = jnp.where(jnp.broadcast_to(direction, square) == imag_ids, 1.0, 0.0).astype(BF16)
    row_half = lax.rem(r // pad, 2)

    for copy in plane_copies:
        copy.wait_recv()
    whole = gathered[...]
    panel_real = dot(pick_real, whole)
    panel_imag = dot(pick_imag, whole)
    panel_power = (panel_real * panel_real + panel_imag * panel_imag).astype(BF16)
    norm = by_group(dot_t(panel_power, tables[1]), 1)
    scores = (
        dot_t(panel_real.astype(BF16), weighted[:, :PIXC])
        + dot_t(panel_imag.astype(BF16), weighted[:, PIXC:])
        - 0.5 * dot(norm, onehot[...])
    )
    use = (prior[...] > 0) & (halves[...] == row_half) & (slot < rows)
    masked = jnp.where(use, scores, -1e30)
    local_peak = jnp.max(masked, axis=0, keepdims=True)
    raw = jnp.where(use, jnp.exp(masked - local_peak), 0.0)
    local_total = jnp.sum(raw, axis=0, keepdims=True)
    peaks[0, 0:1, :] = local_peak
    peaks[0, 1:2, :] = local_total
    class_copies = []
    for i in range(1, ncls):
        copy = remote(
            peaks.at[0],
            peaks.at[i],
            csend.at[i],
            crecv.at[i],
            cls=lax.rem(mine + i, ncls),
        )
        copy.start()
        class_copies.append(copy)
    for copy in class_copies:
        copy.wait_recv()
    peak = local_peak
    for i in range(1, ncls):
        peak = jnp.maximum(peak, peaks[i, 0:1, :])
    total = local_total * jnp.exp(local_peak - peak)
    for i in range(1, ncls):
        total = total + peaks[i, 1:2, :] * jnp.exp(peaks[i, 0:1, :] - peak)
    posts[...] = (raw * (jnp.exp(local_peak - peak) / total)).astype(BF16)
    evidence[...] = peak + jnp.log(total)

    plane_sends = []
    for k, (start, width) in enumerate(CHUNKS):
        data_width = min(width, 2 * PIXC - start)
        part = dot(posts[...], centred[:, start : start + data_width])
        acc[:, start : start + data_width] = part[:own_rows]
        send1[:, start : start + data_width] = part[own_rows:].astype(BF16)
        if data_width < width:
            sums = dot_t(posts[...], onehot[...])
            acc[:, 2 * PIXC :] = jnp.where(
                iota((own_rows, LANES), 1) < NBIN, sums[:own_rows], 0.0
            )
            send1[:, 2 * PIXC :] = by_group(sums[own_rows:], 1)
        cols = pl.ds(start, width)
        group = []
        for p in range(1, plane):
            copy = remote(
                send1.at[pl.ds((p - 1) * own_rows, own_rows), cols],
                recv1.at[p - 1, :, cols],
                s1send.at[k, p],
                s1recv.at[k, p],
                at(l, lax.rem(q + p, plane)),
            )
            copy.start()
            group.append(copy)
        plane_sends.append(group)

    line_sends = []
    for k, (start, width) in enumerate(CHUNKS):
        cols = pl.ds(start, width)
        for copy in plane_sends[k]:
            copy.wait_recv()
        value = acc[:, start : start + width]
        for p in range(1, plane):
            value = value + recv1[p - 1, :, start : start + width].astype(F32)
        acc[:, start : start + width] = value
        group = []
        for i in range(1, line):
            copy = remote(
                acc.at[pl.ds(i * block, block), cols],
                recv2.at[i - 1, :, cols],
                s2send.at[k, i],
                s2recv.at[k, i],
                at(lax.rem(l + i, line), q),
            )
            copy.start()
            group.append(copy)
        line_sends.append(group)

    for k, (start, width) in enumerate(CHUNKS):
        for copy in line_sends[k]:
            copy.wait_recv()
        value = acc[:block, start : start + width]
        for i in range(1, line):
            value = value + recv2[i - 1, :, start : start + width]
        final[0, :, start : start + width] = value[:pad]
        final[1, :, start : start + width] = value[pad:]

    swap = remote(
        final.at[1 - half],
        swapped.at[half],
        xsend,
        xrecv,
        lax.rem(me + n // 2, n),
    )
    swap.start()
    first = final[0, :, : 2 * PIXC]
    second = final[1, :, : 2 * PIXC]

    def folded(values):
        summed = jnp.sum(values, axis=0, keepdims=True)
        return summed[:, :PIXC] + summed[:, PIXC:]

    table_rows = jnp.concatenate(
        [
            folded(first * second),
            folded(first * first),
            folded(second * second),
            jnp.zeros((5, PIXC), F32),
        ],
        axis=0,
    )
    stats[0] = exact(table_rows, lambda v: dot_t(v, shell_pick))
    stat_copies = []
    for i in range(1, n):
        copy = remote(
            stats.at[0], stats.at[i], tsend.at[i], trecv.at[i], lax.rem(me + i, n)
        )
        copy.start()
        stat_copies.append(copy)
    kept = final[half]
    swap.wait_recv()
    swapped[half] = kept
    ready = []
    for h in range(2):
        bin_sums = swapped[h, :, 2 * PIXC :]
        ready.append(1.0 + exact(bin_sums, lambda v: dot(v, tables[2])))
    for copy in stat_copies:
        copy.wait_recv()
    sums = stats[0]
    for i in range(1, n):
        sums = sums + stats[i]
    fsc = sums[0:1] / jnp.sqrt(sums[1:2] * sums[2:3] + 1e-06)
    factor = jnp.broadcast_to((1.0 + fsc) / 2.0, (8, LANES))
    factor = exact(factor, lambda v: dot(v, shell_pick))[0:1, :]
    for h in range(2):
        for part in range(2):
            cols = slice(part * PIXC, (part + 1) * PIXC)
            value = swapped[h, :, cols] * factor / ready[h]
            maps[0, h * rows : (h + 1) * rows, cols] = value[:rows]

    for copy in line_copies[1:] + plane_copies + class_copies + stat_copies + [swap]:
        copy.wait_send()
    for group in plane_sends + line_sends:
        for copy in group:
            copy.wait_send()


def solution(mesh):
    n = mesh.shape["ptcl"]
    ncls = mesh.shape["cls"]
    plane = 4
    line = n // plane
    rows = ORIENT // n
    pad = max(8, rows)
    block = 2 * pad
    own_rows = line * block
    nchunks = len(CHUNKS)

    def on_device(particles, panels, sigma2, defocus_bins, half_sets, prior_mask, orient_ids):
        count = particles.shape[0]
        dims = (n, ncls, plane, line, rows, pad, count)
        vmem = pl.BlockSpec(memory_space=pltpu.VMEM)
        dma = pltpu.SemaphoreType.DMA
        maps, evidence = pl.pallas_call(
            functools.partial(kernel, dims),
            out_shape=(
                jax.ShapeDtypeStruct((1, 2 * rows, 2 * PIXC), F32),
                jax.ShapeDtypeStruct((1, count), F32),
            ),
            in_specs=[pl.BlockSpec(memory_space=pl.ANY)] + [vmem] * 7,
            out_specs=(vmem, vmem),
            scratch_shapes=[
                pltpu.VMEM((count, 2 * PIXC), BF16),
                pltpu.VMEM((count, 2 * PIXC), BF16),
                pltpu.VMEM((count, 2 * PIXC), BF16),
                pltpu.VMEM((n * block, PIXC), BF16),
                pltpu.VMEM((LANES, count), BF16),
                pltpu.VMEM((3, LANES, PIXC), BF16),
                pltpu.VMEM((8, PIXC), F32),
                pltpu.VMEM((ncls, 2, count), F32),
                pltpu.VMEM((n * block, count), BF16),
                pltpu.VMEM((n * block - own_rows, WIDTH), BF16),
                pltpu.VMEM((plane - 1, own_rows, WIDTH), BF16),
                pltpu.VMEM((own_rows, WIDTH), F32),
                pltpu.VMEM((line - 1, block, WIDTH), F32),
                pltpu.VMEM((2, pad, WIDTH), F32),
                pltpu.VMEM((2, pad, WIDTH), F32),
                pltpu.VMEM((n, 8, LANES), F32),
                dma((4,)),
                dma((line, plane)),
                dma((line, plane)),
                dma((ncls,)),
                dma((ncls,)),
                dma((nchunks, plane)),
                dma((nchunks, plane)),
                dma((nchunks, line)),
                dma((nchunks, line)),
                dma,
                dma,
                dma((n,)),
                dma((n,)),
            ],
            compiler_params=pltpu.CompilerParams(
                collective_id=0, has_side_effects=True, vmem_limit_bytes=56 * 2**20
            ),
        )(
            particles,
            panels,
            sigma2.reshape(1, NSHELL),
            defocus_bins.reshape(1, count),
            half_sets.reshape(1, count),
            prior_mask.reshape(1, count),
            orient_ids.reshape(1, ORIENT),
            jnp.asarray(ctf_table()),
        )
        return maps, evidence.reshape(count)

    return jax.shard_map(
        on_device,
        mesh=mesh,
        in_specs=(
            P("ptcl", None),
            P("cls", "ptcl", None),
            P(),
            P("ptcl"),
            P("ptcl"),
            P("ptcl", "cls"),
            P(),
        ),
        out_specs=(P("cls", "ptcl", None), P("ptcl")),
        check_vma=False,
    )
```

time: 262 us -> 51.5 us (0.20)
  waiting for transfers between devices: 129 us -> 0 us
  blocking collectives: 90.3 us -> 0 us
  Pallas kernels: 0 us -> 47.8 us
  between operations: 14.2 us -> 0.64 us
  matrix products: 10.4 us -> 0 us
  other arithmetic: 7.76 us -> 0 us
  local copies, waits for them, and re-layouts: 8.34 us -> 2.85 us
    reduce_scatter x1 -> x0, waiting for transfers between devices: 127 us -> none  [on_device(): lax.psum_scatter(contract_rows(split_post, stacked), 'ptcl', scatter_dime...]
    pallas_call x0 -> x1, Pallas kernels: none -> 47.8 us  [on_device(): pl.pallas_call(functools.partial(kernel, dims), out_shape=(jax.ShapeDtype...]
    all_gather x1 -> x0, blocking collectives: 45.5 us -> none  [on_device(): piece = lax.all_gather(panels[0], 'ptcl', axis=0, tiled=True)]
    psum x2 -> x0, blocking collectives: 42.3 us -> none  [the longest x1 39.8 us: on_device(): totals = lax.psum(stats, 'ptcl')]
    dot_general x5 -> x0, matrix products: 10.4 us -> none  [the longest x1 5.75 us: contract_rows(): lax.dot_general(left, right, (((0,), (0,)), ((), ())), preferred_element_...]
    unnamed x13 -> x2, local copies, waits for them, and re-layouts: 6.44 us -> 2.85 us
    convert_element_type x2 -> x0, other arithmetic: 3.35 us -> none  [the longest x1 3.25 us: on_device(): centred = (images * doubled).astype(jnp.bfloat16)]
  transfers between devices with their start and end apart: 2 -> 0, of which waited for: 2 -> 0; matrix products, arithmetic and copies ran while one was open for 1% -> 0% of each run, Pallas kernels for 0% -> 0%
where the time goes in v1:
time: 51.5 us; the launch traced here: 51.3 us
  Pallas kernels  47.8 us (93%)
  local copies, waits for them, and re-layouts  2.85 us (6%)
  between operations  0.64 us (1%)
    pallas_call x1, Pallas kernels, on_device(): pl.pallas_call(functools.partial(kernel, dims), out_shape=(jax.ShapeDtype...  47.8 us
    unnamed x2, local copies, waits for them, and re-layouts  2.85 us

profile of v1, /device:TPU:0, one launch (start us, length us, event | category | flops | bytes accessed | tf_op | source)
XLA Modules:
  0.0 51.3 jit_solution(3014124596788432679)
XLA Ops:
  0.6 47.8 %shard_map.95 = (f32[1,16,2048]{2,1,0:T(8,128)}, f32[1,1024]{1,0:T(1,128)}) custom-call(bf16[1024,2048]{1,0:T(8,128)(2,1)} %particles.1, bf16[1,8,2048]{2,1,0:T(8,128)(2,1)} %panels.1, f32[1,32]{1,0:T(1,128)} %bitcast.10, s32[1,1024]{1,0:T(1,128)} %bitcast.7, s32[1,1024]{1,0:T(1,128)} %bitcast.8, s32[1,1024]{1,0:T(1,128)} %bitcast.9, s32[1,128]{1,0:T(1,128)} %bitcast.11, ...), custom_call_target="tpu_custom_call" | custom-call | tf_op jit(solution)/shard_map/pallas_call | solution.py:436
  48.4 1.6 %copy.12 = f32[1,16,2048]{2,1,0:T(8,128)} copy(f32[1,16,2048]{2,1,0:T(8,128)} %get-tuple-element.8) | data formatting | bytes 262144
  50.0 1.3 %copy.13 = f32[1024]{0:T(1024)} copy(f32[1024]{0:T(1024)} %bitcast.6) | data formatting | bytes 8192
